TPU v7x, 512 devices: a whole 4x8x8 slice. The times are simulated.
512 devices in a mesh: row: 128 (over y, z, core), lm: 4 (over x).
Axes of the slice: x: 4, y: 8, z: 8, core: 2. Of those that a mesh axis runs over, the one named last changes fastest.
Arguments:
- state: float32 [3, 2048, 1024], P(None, 'row', 'lm'), may hold values from -6 to 6
- previous_terms: float32 [3, 2048, 1024], P(None, 'row', 'lm'), may hold values from -6 to 6
- below: float32 [2, 3, 1024], P(None, None, 'lm'), may hold values from -6 to 6
- above: float32 [2, 3, 1024], P(None, None, 'lm'), may hold values from -6 to 6
- kappa: float32 [3], replicated, may hold values from 0.25 to 1
Outputs:
- new_state: float32 [3, 2048, 1024], P(None, 'row', 'lm')
- nonlinear: float32 [3, 2048, 1024], P(None, 'row', 'lm')
All inputs are finite; a program needn't handle non-finite values.
Results may differ from a plain program's by a relative error of at most 0.0006.
Values sent between devices are 32-bit elements; how exact they have to be, the bound alone decides.
A program may use at most 64 MiB of HBM per device.

v0:
```python
import functools
import math

import jax
import jax.numpy as jnp
from jax import lax
from jax.experimental import pallas as pl
from jax.experimental.pallas import tpu as pltpu
from jax.sharding import PartitionSpec as P

MESH = pl.DeviceIdType.MESH
F32, BF16 = jnp.float32, jnp.bfloat16
NLAT = 1536
HALF = NLAT // 2
DEGREES = 1024
PAIRS = DEGREES // 2
SHELLS = 2048
SHELLS_DEV = 16
CHIP = 2 * SHELLS_DEV
FIELDS = 3
TILE = (8, 128)
CENTRAL_TERMS = [math.comb(2 * k, k) / 4.0**k for k in range(16)]


def central_ratio(counts):
    number = counts.astype(F32)
    bigger = jnp.maximum(number, 1.0)
    inverse = 1.0 / bigger
    series = 1.0 + inverse * (
        -0.125 + inverse * (0.0078125 + inverse * (0.0048828125 - inverse * 0.000640869140625))
    )
    result = series * lax.rsqrt(math.pi * bigger)
    for k in range(16):
        result = jnp.where(counts == k, CENTRAL_TERMS[k], result)
    return jnp.where(counts < 0, 0.0, result)


def cosine(phase):
    turn = 4.0 * NLAT
    number = phase.astype(F32)
    number = number - turn * jnp.floor(number * (1.0 / turn) + 0.5)
    angle = (NLAT - jnp.abs(number)) * (math.pi / (2 * NLAT))
    square = angle * angle
    total = jnp.full_like(square, 1.0 / math.factorial(13))
    for order in (11, 9, 7, 5, 3, 1):
        sign = -1.0 if order % 4 == 3 else 1.0
        total = sign / math.factorial(order) + square * total
    return angle * total


def split2(value):
    high = value.astype(BF16)
    low = (value - high.astype(F32)).astype(BF16)
    return high, low


def dot(left, right, transposed=False):
    dims = (((1,), (1 if transposed else 0,)), ((), ()))
    return lax.dot_general(left, right, dims, preferred_element_type=F32)


def dot3(left, high, low, transposed=False):
    rows = left.shape[0]
    top, rest = split2(left)
    both = dot(jnp.concatenate([top, rest], axis=0), high, transposed)
    return both[:rows] + both[rows:] + dot(top, low, transposed)


def permute_lanes(value, matrix):
    rows = value.shape[0]
    first = value.astype(BF16)
    left = value - first.astype(F32)
    second = left.astype(BF16)
    third = (left - second.astype(F32)).astype(BF16)
    out = dot(jnp.concatenate([first, second, third], axis=0), matrix)
    return out[:rows] + out[rows : 2 * rows] + out[2 * rows :]


def iota(shape, axis):
    return lax.broadcasted_iota(jnp.int32, shape, axis)


def level_parts(ports, own):
    count = len(ports)
    one, nothing = jnp.ones(TILE, F32), jnp.zeros(TILE, F32)

    def pick(place, new, old):
        return jnp.where(own == place, new, old)

    forward, backward = [None] * count, [None] * count
    a1, b1 = one, nothing
    pre_a1, pre_b1, thru_a1, thru_b1 = one, nothing, one, nothing
    for k in range(count):
        pa0, pb0, pa1, pb1 = ports[k]
        pre_a1, pre_b1 = pick(k, a1, pre_a1), pick(k, b1, pre_b1)
        beta = pa1 / (1.0 - b1 * pa0)
        forward[k] = (beta, beta * b1)
        a1, b1 = beta * a1, pb1 + beta * b1 * pb0
        thru_a1, thru_b1 = pick(k, a1, thru_a1), pick(k, b1, thru_b1)
    a0, b0 = nothing, one
    post_a0, post_b0, from_a0, from_b0 = nothing, one, nothing, one
    for k in reversed(range(count)):
        pa0, pb0, pa1, pb1 = ports[k]
        post_a0, post_b0 = pick(k, a0, post_a0), pick(k, b0, post_b0)
        gamma = pb0 / (1.0 - pb1 * a0)
        backward[k] = (gamma, gamma * a0)
        a0, b0 = pa0 + gamma * a0 * pa1, gamma * b0
        from_a0, from_b0 = pick(k, a0, from_a0), pick(k, b0, from_b0)
    lower_scale = 1.0 / (1.0 - pre_b1 * from_a0)
    upper_scale = 1.0 / (1.0 - post_a0 * thru_b1)
    lower = (lower_scale * pre_a1, lower_scale * pre_b1 * from_b0, lower_scale * pre_b1, lower_scale)
    upper = (
        upper_scale * post_a0 * thru_a1,
        upper_scale * post_b0,
        upper_scale * post_a0,
        upper_scale,
    )
    return forward, backward, lower, upper, (a0, b0, a1, b1)


def level_constants(parts, constants, own):
    forward, backward, lower, upper, _ = parts
    count = len(forward)
    nothing = jnp.zeros(TILE, F32)

    def pick(place, new, old):
        return jnp.where(own == place, new, old)

    c1, pre, thru = nothing, nothing, nothing
    for k in range(count):
        k0, k1 = constants[k]
        pre = pick(k, c1, pre)
        beta, beta_b = forward[k]
        c1 = (k1 + beta_b * k0) + beta * c1
        thru = pick(k, c1, thru)
    c0, post, start = nothing, nothing, nothing
    for k in reversed(range(count)):
        k0, k1 = constants[k]
        post = pick(k, c0, post)
        gamma, gamma_a = backward[k]
        c0 = (k0 + gamma_a * k1) + gamma * c0
        start = pick(k, c0, start)
    return c0, c1, lower[2] * start + lower[3] * pre, upper[2] * thru + upper[3] * post


def kernel(
    state_hbm,
    previous_hbm,
    below_hbm,
    above_hbm,
    kappa_hbm,
    new_ref,
    nonlinear_ref,
    state_raw,
    previous_raw,
    sides_raw,
    kappa_ref,
    mix,
    wide,
    tri_x,
    sent_x,
    got_x,
    forcing,
    ports_t,
    ports_h,
    exp_high,
    exp_low,
    angle_cos,
    angle_sin,
    cos_high,
    cos_low,
    sent_n,
    got_n,
    radial,
    green,
    solved,
    port_z,
    port_y,
    const_z,
    const_y,
    load_sem,
    x_send,
    x_recv,
    n_send,
    n_recv,
    u_send,
    u_recv,
    pz_send,
    pz_recv,
    py_send,
    py_recv,
    cz_send,
    cz_recv,
    cy_send,
    cy_recv,
):
    row, mode = lax.axis_index("row"), lax.axis_index("lm")
    y, z, core = row // 16, lax.rem(row // 2, 8), lax.rem(row, 2)
    other = row + 1 - 2 * core
    turn = [lax.rem(mode + d, 4) for d in range(4)]
    x_peers = [(row, turn[d]) for d in range(1, 4)]
    core_peers = [(other, turn[d]) for d in range(4)]
    z_peers = [(y * 16 + lax.rem(z + d, 8) * 2 + core, mode) for d in (4, 3, 5, 2, 6, 1, 7)]
    y_peers = [(lax.rem(y + d, 8) * 16 + z * 2 + core, mode) for d in (4, 3, 5, 2, 6, 1, 7)]

    barrier = pltpu.get_barrier_semaphore()
    everyone = z_peers + y_peers + x_peers + core_peers
    for peer in everyone:
        pl.semaphore_signal(barrier, inc=1, device_id=peer, device_id_type=MESH)

    loads = [
        pltpu.make_async_copy(state_hbm, state_raw, load_sem.at[0]),
        pltpu.make_async_copy(previous_hbm, previous_raw, load_sem.at[1]),
        pltpu.make_async_copy(below_hbm, sides_raw.at[0], load_sem.at[2]),
        pltpu.make_async_copy(above_hbm, sides_raw.at[1], load_sem.at[3]),
        pltpu.make_async_copy(kappa_hbm, kappa_ref, load_sem.at[4]),
    ]
    for load in loads:
        load.start()

    def send(source, target, send_sem, recv_sem, peer):
        copy = pltpu.make_async_remote_copy(
            src_ref=source,
            dst_ref=target,
            send_sem=send_sem,
            recv_sem=recv_sem,
            device_id=peer,
            device_id_type=MESH,
        )
        copy.start()
        return copy

    source_id, target_id = iota((256, 256), 0), iota((256, 256), 1)
    part = (source_id == 2 * (target_id & 127) + (target_id >> 7)).astype(F32).astype(BF16)
    unite = (target_id == 2 * (source_id & 127) + (source_id >> 7)).astype(F32).astype(BF16)
    sub, lane = iota(TILE, 0), iota(TILE, 1)
    parity, field = sub >> 2, sub & 3
    degree = (mode * 256 + 2 * lane + parity).astype(F32)
    scale = jnp.sqrt(degree + 0.5)

    def to_tiles(values, target):
        for f in range(FIELDS):
            for p in range(2):
                target[pl.ds(p * 4 + f, SHELLS_DEV, stride=8), :] = values[
                    f * 16 : (f + 1) * 16, p * 128 : (p + 1) * 128
                ]

    def from_tiles(source):
        return jnp.concatenate(
            [
                jnp.concatenate(
                    [source[pl.ds(p * 4 + f, SHELLS_DEV, stride=8), :] for p in range(2)], axis=1
                )
                for f in range(FIELDS)
            ],
            axis=0,
        )

    tri_x[...] = jnp.zeros_like(tri_x)
    wide[...] = jnp.zeros_like(wide)
    loads[0].wait()
    to_tiles(permute_lanes(state_raw[...].reshape(48, 256), part), tri_x)
    sent_x[...] = tri_x[...].reshape(SHELLS_DEV, 8, 128) * scale
    pl.semaphore_wait(barrier, len(everyone))
    copies_x = [
        send(
            sent_x.at[pl.ds(peer[1] * 4, 4)],
            got_x.at[mode],
            x_send.at[d],
            x_recv.at[d],
            peer,
        )
        for d, peer in enumerate(x_peers)
    ]
    got_x[mode] = sent_x[pl.ds(mode * 4, 4)]

    loads[1].wait()
    to_tiles(permute_lanes(previous_raw[...].reshape(48, 256), part), wide)
    push = 4.0 * SHELLS_DEV * SHELLS_DEV
    forcing[pl.ds(core * SHELLS_DEV, SHELLS_DEV)] = (
        2.0 * tri_x[...] - (0.5 * push) * wide[...]
    ).reshape(SHELLS_DEV, 8, 128)
    copy_u = send(
        forcing.at[pl.ds(core * SHELLS_DEV, SHELLS_DEV)],
        forcing.at[pl.ds(core * SHELLS_DEV, SHELLS_DEV)],
        u_send.at[0],
        u_recv.at[0],
        core_peers[0],
    )

    toeplitz = central_ratio(512 + iota((8, 640), 0) - iota((8, 640), 1))
    hankel = [central_ratio(iota((8, 1024), 0) + iota((8, 1024), 1) + p) for p in range(2)]
    for step in range(16):
        rows = slice(step * 8, step * 8 + 8)
        moved = toeplitz if step == 0 else pltpu.roll(toeplitz, step * 8, 1)
        for b in range(4):
            ports_t[b, rows, :] = moved[:, (4 - b) * 128 : (5 - b) * 128]
        for p in range(2):
            moved = hankel[p] if step == 0 else pltpu.roll(hankel[p], 1024 - step * 8, 1)
            for b in range(7):
                ports_h[p, b, rows, :] = moved[:, b * 128 : (b + 1) * 128]
    for p in range(2):
        for a in range(4):
            for b in range(4):
                here = (p, slice(a * 128, a * 128 + 128), slice(b * 128, b * 128 + 128))
                if b <= a:
                    high, low = split2(ports_t[a - b] * ports_h[p, a + b])
                else:
                    high = low = jnp.zeros((128, 128), BF16)
                exp_high[here] = high
                exp_low[here] = low

    def phase(order, shape):
        return order * (2 * iota(shape, 1) + 1)

    wide_shape = (8, HALF)
    for p, groups in ((0, 7), (1, 4)):
        for group in range(groups):
            turns = phase(32 * (group * 8 + iota(wide_shape, 0)) + p, wide_shape)
            angle_cos[p, group * 8 : group * 8 + 8, :] = 2.0 * cosine(turns)
            angle_sin[p, group * 8 : group * 8 + 8, :] = 2.0 * cosine(turns - NLAT)
    base_shape = (16, HALF)
    turns = phase(2 * iota(base_shape, 0), base_shape)
    base_cos, base_sin = cosine(turns), cosine(turns - NLAT)
    base_row = iota((16, 128), 0)

    def series_term(q):
        order = (16 * q + base_row).astype(F32)
        term = -1.0 / (4.0 * order * order - 1.0)
        term = jnp.where(order > HALF, 0.0, term)
        return jnp.concatenate([term] * (HALF // 128), axis=1)

    def table_rows(p, q):
        return (
            angle_cos[p, pl.ds(q, 1), :] * base_cos - angle_sin[p, pl.ds(q, 1), :] * base_sin
        )

    def fill(q, weight):
        for p in range(2):
            values = table_rows(p, q)
            if p == 0:
                values = jnp.where((iota(base_shape, 0) + 16 * q) == 0, 1.0, values)
                weight = weight + series_term(q) * values
            high, low = split2(values)
            where = pl.ds(pl.multiple_of(q * 16, 16), 16)
            cos_high[p, where, :] = high
            cos_low[p, where, :] = low
        return weight

    weight = lax.fori_loop(0, 32, fill, jnp.zeros(base_shape, F32))
    weight = lax.fori_loop(
        32, 49, lambda q, weight: weight + series_term(q) * table_rows(0, q), weight
    )
    weight = jnp.sum(weight, axis=0, keepdims=True) * (2.0 / NLAT / 16.0)

    for copy in copies_x:
        copy.wait_recv()
    even_rows = (iota((32, 1), 0) & 4) == 0
    field_rows = iota((32, 1), 0) & 3
    sign = jnp.where(even_rows, 1.0, -1.0)

    def parities(left, right):
        return jnp.where(even_rows, left, right)

    def swap(values):
        return pltpu.roll(values.reshape(4, 8, values.shape[1]), 4, 1).reshape(values.shape)

    def rolled(values, shift):
        return pltpu.roll(values.reshape(4, 8, values.shape[1]), shift, 1).reshape(values.shape)

    spectrum = jnp.concatenate([got_x[k].reshape(32, 128) for k in range(4)], axis=1)
    half = PAIRS // 2

    def expand(p):
        first = dot3(spectrum, exp_high[p, :, :half], exp_low[p, :, :half])
        second = dot3(spectrum[:, half:], exp_high[p, half:, half:], exp_low[p, half:, half:])
        return jnp.concatenate([first, second], axis=1)

    orders = parities(expand(0), expand(1))
    sides = parities(*[dot3(orders, cos_high[p], cos_low[p]) for p in range(2)])
    grid = swap(sides) + sign * sides
    after, before, twice = rolled(grid, 7), rolled(grid, 1), rolled(grid, 2)
    product = jnp.where(
        field_rows == 0,
        after * after - grid * grid,
        jnp.where(field_rows == 1, before * grid, jnp.where(field_rows == 2, -(twice * grid), 0.0)),
    )
    product = product * weight
    folded = swap(product) + sign * product
    orders = parities(*[dot3(folded, cos_high[p], cos_low[p], True) for p in range(2)])

    def contract(p):
        first = dot3(orders[:, :half], exp_high[p, :half, :half], exp_low[p, :half, :half], True)
        second = dot3(orders, exp_high[p, half:, :], exp_low[p, half:, :], True)
        return jnp.concatenate([first, second], axis=1)

    terms = parities(contract(0), contract(1))
    for k in range(4):
        sent_n[k] = terms[:, k * 128 : (k + 1) * 128].reshape(4, 8, 128)
    mine = core * 4 + mode
    copies_n = [
        send(sent_n.at[peer[1]], got_n.at[mine], n_send.at[d], n_recv.at[d], peer)
        for d, peer in enumerate(x_peers + core_peers)
    ]
    got_n[mine] = sent_n[mode]

    loads[4].wait()
    kappa = jnp.full(TILE, 1.0, F32)
    for f in range(FIELDS):
        kappa = jnp.where(field == f, kappa_ref[f], kappa)
    spread = kappa * (16.0 * SHELLS_DEV * SHELLS_DEV)
    damping = kappa * (degree * (degree + 1.0)) * (1.0 / 256.0)
    first_shell = (row // 2) * CHIP
    for s in range(CHIP):
        number = jnp.full(TILE, (first_shell + s).astype(F32), F32)
        inverse = 1.0 / (0.5 + (number + 0.5) / (2.0 * SHELLS))
        slope = spread * (inverse * (1.0 / (2.0 * SHELLS)))
        radial[0, s] = (1.0 + 2.0 * spread) + damping * inverse * inverse
        radial[1, s] = spread - slope
        radial[2, s] = spread + slope
    cp, cq = jnp.zeros(TILE, F32), jnp.zeros(TILE, F32)
    for s in range(CHIP):
        t = CHIP - 1 - s
        ip = 1.0 / (radial[0, s] - radial[1, s] * cp)
        cp = radial[2, s] * ip
        radial[3, s], radial[4, s] = cp, ip
        iq = 1.0 / (radial[0, t] - radial[2, t] * cq)
        cq = radial[1, t] * iq
        radial[5, t], radial[6, t] = cq, iq
    low_run = up_run = head_run = tail_run = jnp.ones(TILE, F32)
    for s in range(CHIP):
        t = CHIP - 1 - s
        iq, ip = radial[6, s], radial[4, t]
        green[0, s] = iq * head_run
        head_run = head_run * (radial[2, s] * iq)
        low_run = low_run * radial[5, s]
        green[2, s] = low_run
        green[1, t] = ip * tail_run
        tail_run = tail_run * (radial[1, t] * ip)
        up_run = up_run * radial[3, t]
        green[3, t] = up_run
    port_z[z, 0], port_z[z, 1] = green[2, 0], green[3, 0]
    port_z[z, 2], port_z[z, 3] = green[2, CHIP - 1], green[3, CHIP - 1]
    copies_pz = [
        send(port_z.at[z], port_z.at[z], pz_send.at[d], pz_recv.at[d], peer)
        for d, peer in enumerate(z_peers)
    ]

    loads[2].wait()
    loads[3].wait()
    mix[...] = jnp.zeros_like(mix)
    for k in range(2):
        mix[k * 8 : k * 8 + FIELDS, :] = sides_raw[k, 0] + sides_raw[k, 1]
    parted = permute_lanes(mix[...], part)
    bottom, top = [
        jnp.concatenate([parted[k * 8 : k * 8 + 4, :128], parted[k * 8 : k * 8 + 4, 128:]], axis=0)
        for k in range(2)
    ]

    copy_u.wait_recv()
    for copy in copies_n:
        copy.wait_recv()
    factor = (1.5 * push) * scale
    sums = [[None] * 4, [None] * 4]
    for s in range(CHIP):
        value = forcing[s] + factor * got_n[s // 4, s % 4]
        solved[s] = value
        for k in range(2):
            term = green[k, s] * value
            old = sums[k][s % 4]
            sums[k][s % 4] = term if old is None else old + term
    for k in range(2):
        const_z[z, k] = (sums[k][0] + sums[k][1]) + (sums[k][2] + sums[k][3])
    copies_cz = [
        send(const_z.at[z], const_z.at[z], cz_send.at[d], cz_recv.at[d], peer)
        for d, peer in enumerate(z_peers)
    ]

    for copy in copies_pz:
        copy.wait_recv()
    parts_z = level_parts([tuple(port_z[k, m] for m in range(4)) for k in range(8)], z)
    for m in range(4):
        port_y[y, m] = parts_z[4][m]
    copies_py = [
        send(port_y.at[y], port_y.at[y], py_send.at[d], py_recv.at[d], peer)
        for d, peer in enumerate(y_peers)
    ]

    run = jnp.zeros(TILE, F32)
    for s in range(CHIP):
        ip = radial[4, s]
        run = solved[s] * ip + (radial[1, s] * ip) * run
        solved[s] = run
    run = jnp.zeros(TILE, F32)
    for s in reversed(range(CHIP)):
        run = solved[s] + radial[3, s] * run
        solved[s] = run
    for q in range(4):
        wide[q * 32 : (q + 1) * 32, :] = (got_n[core * 4 + q] * scale).reshape(32, 128)
    nonlinear_ref[...] = permute_lanes(from_tiles(wide), unite).reshape(FIELDS, SHELLS_DEV, 256)

    for copy in copies_cz:
        copy.wait_recv()
    total0, total1, lower_z, upper_z = level_constants(
        parts_z, [(const_z[k, 0], const_z[k, 1]) for k in range(8)], z
    )
    const_y[y, 0], const_y[y, 1] = total0, total1
    copies_cy = [
        send(const_y.at[y], const_y.at[y], cy_send.at[d], cy_recv.at[d], peer)
        for d, peer in enumerate(y_peers)
    ]

    for copy in copies_py:
        copy.wait_recv()
    parts_y = level_parts([tuple(port_y[k, m] for m in range(4)) for k in range(8)], y)
    own_shells = pl.ds(core * SHELLS_DEV, SHELLS_DEV)
    rest = solved[own_shells] - tri_x[...].reshape(SHELLS_DEV, 8, 128)
    from_low, from_up = green[2, own_shells], green[3, own_shells]

    for copy in copies_cy:
        copy.wait_recv()
    _, _, lower_y, upper_y = level_constants(
        parts_y, [(const_y[k, 0], const_y[k, 1]) for k in range(8)], y
    )
    line_low = parts_y[2][0] * bottom + parts_y[2][1] * top + lower_y
    line_up = parts_y[3][0] * bottom + parts_y[3][1] * top + upper_y
    chip_low = parts_z[2][0] * line_low + parts_z[2][1] * line_up + lower_z
    chip_up = parts_z[3][0] * line_low + parts_z[3][1] * line_up + upper_z
    wide[...] = (rest + from_low * chip_low + from_up * chip_up).reshape(128, 128)
    new_ref[...] = permute_lanes(from_tiles(wide), unite).reshape(FIELDS, SHELLS_DEV, 256)

    for copy in copies_x + copies_n + [copy_u] + copies_pz + copies_py + copies_cz + copies_cy:
        copy.wait_send()


def local(state, previous_terms, below, above, kappa):
    block = jax.ShapeDtypeStruct(state.shape, F32)
    vmem, dma = pltpu.VMEM, pltpu.SemaphoreType.DMA
    anywhere = pl.BlockSpec(memory_space=pl.ANY)
    inside = pl.BlockSpec(memory_space=pltpu.VMEM)
    scratch = [
        vmem((FIELDS, SHELLS_DEV, 256), F32),
        vmem((FIELDS, SHELLS_DEV, 256), F32),
        vmem((2, 2, FIELDS, 256), F32),
        pltpu.SMEM((FIELDS,), F32),
        vmem((16, 256), F32),
        vmem((128, 128), F32),
        vmem((128, 128), F32),
        vmem((16, 8, 128), F32),
        vmem((4, 4, 8, 128), F32),
        vmem((CHIP, 8, 128), F32),
        vmem((4, 128, 128), F32),
        vmem((2, 7, 128, 128), F32),
        vmem((2, PAIRS, PAIRS), BF16),
        vmem((2, PAIRS, PAIRS), BF16),
        vmem((2, 56, HALF), F32),
        vmem((2, 56, HALF), F32),
        vmem((2, PAIRS, HALF), BF16),
        vmem((2, PAIRS, HALF), BF16),
        vmem((4, 4, 8, 128), F32),
        vmem((8, 4, 8, 128), F32),
        vmem((7, CHIP, 8, 128), F32),
        vmem((4, CHIP, 8, 128), F32),
        vmem((CHIP, 8, 128), F32),
        vmem((8, 4, 8, 128), F32),
        vmem((8, 4, 8, 128), F32),
        vmem((8, 2, 8, 128), F32),
        vmem((8, 2, 8, 128), F32),
        dma((5,)),
        dma((3,)),
        dma((3,)),
        dma((7,)),
        dma((7,)),
        dma((1,)),
        dma((1,)),
    ] + [dma((7,))] * 8
    return pl.pallas_call(
        kernel,
        out_shape=(block, block),
        in_specs=[anywhere] * 5,
        out_specs=(inside, inside),
        scratch_shapes=scratch,
        compiler_params=pltpu.CompilerParams(
            collective_id=0, has_side_effects=True, vmem_limit_bytes=32 * 1024 * 1024
        ),
    )(state, previous_terms, below, above, kappa)


def solution(mesh):
    in_specs = (
        P(None, "row", "lm"),
        P(None, "row", "lm"),
        P(None, None, "lm"),
        P(None, None, "lm"),
        P(),
    )
    out_specs = (P(None, "row", "lm"), P(None, "row", "lm"))
    return jax.shard_map(local, mesh=mesh, in_specs=in_specs, out_specs=out_specs, check_vma=False)
```

profile of v0, /device:TPU:1, one launch (start us, length us, event | category | flops | bytes accessed | tf_op | source)
XLA Modules:
  0.0 39.0 jit_solution(1228232130101234720)
XLA Ops:
  0.6 0.0 copy-start.3
  0.6 0.7 %copy.7.below_hbm = f32[2,3,256]{2,1,0:T(4,128)S(1)} copy(f32[2,3,256]{2,0,1:T(2,128)} %param.7) | data formatting | bytes 12288 | tf_op args[2]
  1.3 0.0 copy-done.3
  1.3 0.0 copy-start.2
  1.4 0.6 %copy-done.2 = f32[3]{0:T(128)S(1)} copy-done((f32[3]{0:T(128)S(1)}, f32[3]{0:T(128)}, u32[]{:S(2)}) %copy-start.2) | copy-done | bytes 36
  2.0 0.0 copy-start
  2.0 0.8 %copy-done = f32[3,16,256]{2,1,0:T(8,128)S(1)} copy-done((f32[3,16,256]{2,1,0:T(8,128)S(1)}, f32[3,16,256]{2,1,0:T(8,128)}, u32[]{:S(2)}) %copy-start) | copy-done | bytes 49176
  2.8 0.0 copy-start.1
  2.8 0.8 %copy-done.1 = f32[3,16,256]{2,1,0:T(8,128)S(1)} copy-done((f32[3,16,256]{2,1,0:T(8,128)S(1)}, f32[3,16,256]{2,1,0:T(8,128)}, u32[]{:S(2)}) %copy-start.1) | copy-done | bytes 49176
  3.6 34.2 %shard_map.68 = (f32[3,16,256]{2,1,0:T(8,128)S(1)}, f32[3,16,256]{2,1,0:T(8,128)S(1)}) custom-call(f32[3,16,256]{2,1,0:T(8,128)S(1)} %copy-done, f32[3,16,256]{2,1,0:T(8,128)S(1)} %copy-done.1, f32[2,3,256]{2,1,0:T(4,128)S(1)} %copy.7.below_hbm, f32[2,3,256]{2,1,0:T(4,128)S(1)} %copy.8.above_hbm, f32[3]{0:T(128)S(1)} %copy-done.2), custom_call_target="tpu_custom_call" | custom-call | tf_op jit(solution)/shard_map/pallas_call | solution.py:577
  37.8 0.6 %copy.11 = f32[3,16,256]{2,1,0:T(8,128)} copy(f32[3,16,256]{2,1,0:T(8,128)S(1)} %get-tuple-element.4) | data formatting | bytes 98304
  38.4 0.6 %copy.12 = f32[3,16,256]{2,1,0:T(8,128)} copy(f32[3,16,256]{2,1,0:T(8,128)S(1)} %get-tuple-element.5) | data formatting | bytes 98304
  (1 shorter events, 0.0 us)
Async XLA Ops:
  0.6 0.7 %copy-start.3 = (f32[2,3,256]{2,0,1:T(2,128)S(1)}, f32[2,3,256]{2,0,1:T(2,128)}, u32[]{:S(2)}) copy-start(f32[2,3,256]{2,0,1:T(2,128)} %param.8) | copy-start | bytes 18436
  1.3 0.7 %copy-start.2 = (f32[3]{0:T(128)S(1)}, f32[3]{0:T(128)}, u32[]{:S(2)}) copy-start(f32[3]{0:T(128)} %kappa_hbm.1) | copy-start | bytes 40
  2.0 0.8 %copy-start = (f32[3,16,256]{2,1,0:T(8,128)S(1)}, f32[3,16,256]{2,1,0:T(8,128)}, u32[]{:S(2)}) copy-start(f32[3,16,256]{2,1,0:T(8,128)} %state_hbm.1) | copy-start | bytes 147460
  2.8 0.8 %copy-start.1 = (f32[3,16,256]{2,1,0:T(8,128)S(1)}, f32[3,16,256]{2,1,0:T(8,128)}, u32[]{:S(2)}) copy-start(f32[3,16,256]{2,1,0:T(8,128)} %previous_hbm.1) | copy-start | bytes 147460
where the time goes:
time: 39.3 us; the launch traced here: 39 us
  Pallas kernels  34.2 us (87%)
  local copies, waits for them, and re-layouts  4.19 us (11%)
  between operations  0.65 us (2%)
    pallas_call x1, Pallas kernels, local(): pl.pallas_call(kernel, out_shape=(block, block), in_specs=[anywhere] * 5,...  34.2 us
    unnamed x12, local copies, waits for them, and re-layouts  4.19 us

commit v1 on v0

--- a/solution.py
+++ b/solution.py
@@ -230,6 +230,10 @@
         copy.start()
         return copy
 
+    def receive(copies):
+        for copy in copies:
+            copy.wait_recv()
+
     source_id, target_id = iota((256, 256), 0), iota((256, 256), 1)
     part = (source_id == 2 * (target_id & 127) + (target_id >> 7)).astype(F32).astype(BF16)
     unite = (target_id == 2 * (source_id & 127) + (source_id >> 7)).astype(F32).astype(BF16)
@@ -353,8 +357,7 @@
     )
     weight = jnp.sum(weight, axis=0, keepdims=True) * (2.0 / NLAT / 16.0)
 
-    for copy in copies_x:
-        copy.wait_recv()
+    receive(copies_x)
     even_rows = (iota((32, 1), 0) & 4) == 0
     field_rows = iota((32, 1), 0) & 3
     sign = jnp.where(even_rows, 1.0, -1.0)
@@ -450,16 +453,15 @@
     loads[3].wait()
     mix[...] = jnp.zeros_like(mix)
     for k in range(2):
-        mix[k * 8 : k * 8 + FIELDS, :] = sides_raw[k, 0] + sides_raw[k, 1]
+        mix[k * 8 : k * 8 + FIELDS, :] = sides_raw[k, :, 0] + sides_raw[k, :, 1]
     parted = permute_lanes(mix[...], part)
     bottom, top = [
         jnp.concatenate([parted[k * 8 : k * 8 + 4, :128], parted[k * 8 : k * 8 + 4, 128:]], axis=0)
         for k in range(2)
     ]
 
-    copy_u.wait_recv()
-    for copy in copies_n:
-        copy.wait_recv()
+    receive([copy_u])
+    receive(copies_n)
     factor = (1.5 * push) * scale
     sums = [[None] * 4, [None] * 4]
     for s in range(CHIP):
@@ -476,8 +478,7 @@
         for d, peer in enumerate(z_peers)
     ]
 
-    for copy in copies_pz:
-        copy.wait_recv()
+    receive(copies_pz)
     parts_z = level_parts([tuple(port_z[k, m] for m in range(4)) for k in range(8)], z)
     for m in range(4):
         port_y[y, m] = parts_z[4][m]
@@ -499,8 +500,7 @@
         wide[q * 32 : (q + 1) * 32, :] = (got_n[core * 4 + q] * scale).reshape(32, 128)
     nonlinear_ref[...] = permute_lanes(from_tiles(wide), unite).reshape(FIELDS, SHELLS_DEV, 256)
 
-    for copy in copies_cz:
-        copy.wait_recv()
+    receive(copies_cz)
     total0, total1, lower_z, upper_z = level_constants(
         parts_z, [(const_z[k, 0], const_z[k, 1]) for k in range(8)], z
     )
@@ -510,15 +510,13 @@
         for d, peer in enumerate(y_peers)
     ]
 
-    for copy in copies_py:
-        copy.wait_recv()
+    receive(copies_py)
     parts_y = level_parts([tuple(port_y[k, m] for m in range(4)) for k in range(8)], y)
     own_shells = pl.ds(core * SHELLS_DEV, SHELLS_DEV)
     rest = solved[own_shells] - tri_x[...].reshape(SHELLS_DEV, 8, 128)
     from_low, from_up = green[2, own_shells], green[3, own_shells]
 
-    for copy in copies_cy:
-        copy.wait_recv()
+    receive(copies_cy)
     _, _, lower_y, upper_y = level_constants(
         parts_y, [(const_y[k, 0], const_y[k, 1]) for k in range(8)], y
     )
@@ -531,6 +529,17 @@
 
     for copy in copies_x + copies_n + [copy_u] + copies_pz + copies_py + copies_cz + copies_cy:
         copy.wait_send()
+
+
+def write_out(new_ref, nonlinear_ref, new_hbm, nonlinear_hbm, sem):
+    copies = [
+        pltpu.make_async_copy(new_ref, new_hbm, sem.at[0]),
+        pltpu.make_async_copy(nonlinear_ref, nonlinear_hbm, sem.at[1]),
+    ]
+    for copy in copies:
+        copy.start()
+    for copy in copies:
+        copy.wait()
 
 
 def local(state, previous_terms, below, above, kappa):
@@ -541,7 +550,7 @@
     scratch = [
         vmem((FIELDS, SHELLS_DEV, 256), F32),
         vmem((FIELDS, SHELLS_DEV, 256), F32),
-        vmem((2, 2, FIELDS, 256), F32),
+        vmem((2, FIELDS, 2, 256), F32),
         pltpu.SMEM((FIELDS,), F32),
         vmem((16, 256), F32),
         vmem((128, 128), F32),
@@ -574,16 +583,34 @@
         dma((1,)),
         dma((1,)),
     ] + [dma((7,))] * 8
-    return pl.pallas_call(
+    held = pltpu.VMEM(state.shape, F32)
+    operands = [
+        pltpu.with_memory_space_constraint(operand, pltpu.HBM)
+        for operand in (
+            state,
+            previous_terms,
+            jnp.transpose(below, (1, 0, 2)),
+            jnp.transpose(above, (1, 0, 2)),
+            kappa,
+        )
+    ]
+    results = pl.pallas_call(
         kernel,
-        out_shape=(block, block),
+        out_shape=(held, held),
         in_specs=[anywhere] * 5,
         out_specs=(inside, inside),
         scratch_shapes=scratch,
         compiler_params=pltpu.CompilerParams(
             collective_id=0, has_side_effects=True, vmem_limit_bytes=32 * 1024 * 1024
         ),
-    )(state, previous_terms, below, above, kappa)
+    )(*operands)
+    return pl.pallas_call(
+        write_out,
+        out_shape=(block, block),
+        in_specs=[inside] * 2,
+        out_specs=(anywhere, anywhere),
+        scratch_shapes=[dma((2,))],
+    )(*[pltpu.with_memory_space_constraint(result, pltpu.VMEM) for result in results])
 
 
 def solution(mesh):

time: 39.3 us -> 35.7 us (0.908)
  local copies, waits for them, and re-layouts: 4.19 us -> 0 us
  Pallas kernels: 34.2 us -> 34.8 us
    unnamed x12 -> x0, local copies, waits for them, and re-layouts: 4.19 us -> none
    pallas_call x1 -> x2, Pallas kernels: 34.2 us -> 34.8 us  [the longest x1 34.2 us: local(): pl.pallas_call(kernel, out_shape=(held, held), in_specs=[anywhere] * 5, o...]
where the time goes in v1:
time: 35.7 us; the launch traced here: 35.5 us
  Pallas kernels  34.8 us (97%)
  between operations  0.64 us (2%)
    pallas_call x1, Pallas kernels, local(): pl.pallas_call(kernel, out_shape=(held, held), in_specs=[anywhere] * 5, o...  34.2 us

profile of v1, /device:TPU:1, one launch (start us, length us, event | category | flops | bytes accessed | tf_op | source)
XLA Modules:
  0.0 35.5 jit_solution(5533699222480227639)
XLA Ops:
  0.6 34.2 %shard_map.68 = (f32[3,16,256]{2,1,0:T(8,128)S(1)}, f32[3,16,256]{2,1,0:T(8,128)S(1)}) custom-call(f32[3,16,256]{2,1,0:T(8,128)} %state_hbm.1, f32[3,16,256]{2,1,0:T(8,128)} %previous_hbm.1, f32[3,2,256]{2,1,0:T(2,128)} %bitcast.2, f32[3,2,256]{2,1,0:T(2,128)} %bitcast.3, f32[3]{0:T(128)} %kappa_hbm.1), custom_call_target="tpu_custom_call" | custom-call | tf_op jit(solution)/shard_map/pallas_call | solution.py:597
  34.8 0.7 %shard_map.69 = (f32[3,16,256]{2,1,0:T(8,128)}, f32[3,16,256]{2,1,0:T(8,128)}) custom-call(f32[3,16,256]{2,1,0:T(8,128)S(1)} %get-tuple-element.4.new_ref, f32[3,16,256]{2,1,0:T(8,128)S(1)} %get-tuple-element.5.nonlinear_ref), custom_call_target="tpu_custom_call" | custom-call | tf_op jit(solution)/shard_map/pallas_call | solution.py:607

commit v2 on v1

--- a/solution.py
+++ b/solution.py
@@ -29,7 +29,7 @@
     series = 1.0 + inverse * (
         -0.125 + inverse * (0.0078125 + inverse * (0.0048828125 - inverse * 0.000640869140625))
     )
-    result = series * lax.rsqrt(math.pi * bigger)
+    result = series / jnp.sqrt(math.pi * bigger)
     for k in range(16):
         result = jnp.where(counts == k, CENTRAL_TERMS[k], result)
     return jnp.where(counts < 0, 0.0, result)
@@ -169,15 +169,18 @@
     angle_sin,
     cos_high,
     cos_low,
+    flip_high,
+    flip_low,
     sent_n,
     got_n,
-    radial,
+    shell_q,
+    partial,
     green,
     solved,
-    port_z,
     port_y,
     const_z,
     const_y,
+    relay_sem,
     load_sem,
     x_send,
     x_recv,
@@ -185,8 +188,6 @@
     n_recv,
     u_send,
     u_recv,
-    pz_send,
-    pz_recv,
     py_send,
     py_recv,
     cz_send,
@@ -200,13 +201,6 @@
     turn = [lax.rem(mode + d, 4) for d in range(4)]
     x_peers = [(row, turn[d]) for d in range(1, 4)]
     core_peers = [(other, turn[d]) for d in range(4)]
-    z_peers = [(y * 16 + lax.rem(z + d, 8) * 2 + core, mode) for d in (4, 3, 5, 2, 6, 1, 7)]
-    y_peers = [(lax.rem(y + d, 8) * 16 + z * 2 + core, mode) for d in (4, 3, 5, 2, 6, 1, 7)]
-
-    barrier = pltpu.get_barrier_semaphore()
-    everyone = z_peers + y_peers + x_peers + core_peers
-    for peer in everyone:
-        pl.semaphore_signal(barrier, inc=1, device_id=peer, device_id_type=MESH)
 
     loads = [
         pltpu.make_async_copy(state_hbm, state_raw, load_sem.at[0]),
@@ -217,6 +211,35 @@
     ]
     for load in loads:
         load.start()
+
+    def along_z(d):
+        return (y * 16 + lax.rem(z + d, 8) * 2 + core, mode)
+
+    def along_y(d):
+        return (lax.rem(y + d, 8) * 16 + z * 2 + core, mode)
+
+    z_peers = [along_z(d) for d in (4, 3, 5, 2, 6, 1, 7)]
+    y_peers = [along_y(d) for d in (4, 3, 5, 2, 6, 1, 7)]
+
+    barrier = pltpu.get_barrier_semaphore()
+    near = x_peers + core_peers + [line(d) for line in (along_z, along_y) for d in (1, 7)]
+    for peer in near:
+        pl.semaphore_signal(barrier, inc=1, device_id=peer, device_id_type=MESH)
+
+    def relay(step):
+        for k, line in enumerate((along_z, along_y)):
+            for side, d in enumerate((step, 8 - step)):
+                pl.semaphore_signal(
+                    relay_sem.at[step - 1, k, side],
+                    inc=1,
+                    device_id=line(d),
+                    device_id_type=MESH,
+                )
+
+    def relayed(step):
+        for k in range(2):
+            for side in range(2):
+                pl.semaphore_wait(relay_sem.at[step - 1, k, side], 1)
 
     def send(source, target, send_sem, recv_sem, peer):
         copy = pltpu.make_async_remote_copy(
@@ -259,38 +282,6 @@
             ],
             axis=0,
         )
-
-    tri_x[...] = jnp.zeros_like(tri_x)
-    wide[...] = jnp.zeros_like(wide)
-    loads[0].wait()
-    to_tiles(permute_lanes(state_raw[...].reshape(48, 256), part), tri_x)
-    sent_x[...] = tri_x[...].reshape(SHELLS_DEV, 8, 128) * scale
-    pl.semaphore_wait(barrier, len(everyone))
-    copies_x = [
-        send(
-            sent_x.at[pl.ds(peer[1] * 4, 4)],
-            got_x.at[mode],
-            x_send.at[d],
-            x_recv.at[d],
-            peer,
-        )
-        for d, peer in enumerate(x_peers)
-    ]
-    got_x[mode] = sent_x[pl.ds(mode * 4, 4)]
-
-    loads[1].wait()
-    to_tiles(permute_lanes(previous_raw[...].reshape(48, 256), part), wide)
-    push = 4.0 * SHELLS_DEV * SHELLS_DEV
-    forcing[pl.ds(core * SHELLS_DEV, SHELLS_DEV)] = (
-        2.0 * tri_x[...] - (0.5 * push) * wide[...]
-    ).reshape(SHELLS_DEV, 8, 128)
-    copy_u = send(
-        forcing.at[pl.ds(core * SHELLS_DEV, SHELLS_DEV)],
-        forcing.at[pl.ds(core * SHELLS_DEV, SHELLS_DEV)],
-        u_send.at[0],
-        u_recv.at[0],
-        core_peers[0],
-    )
 
     toeplitz = central_ratio(512 + iota((8, 640), 0) - iota((8, 640), 1))
     hankel = [central_ratio(iota((8, 1024), 0) + iota((8, 1024), 1) + p) for p in range(2)]
@@ -314,6 +305,25 @@
                 exp_high[here] = high
                 exp_low[here] = low
 
+    tri_x[...] = jnp.zeros_like(tri_x)
+    wide[...] = jnp.zeros_like(wide)
+    loads[0].wait()
+    to_tiles(permute_lanes(state_raw[...].reshape(48, 256), part), tri_x)
+    sent_x[...] = tri_x[...].reshape(SHELLS_DEV, 8, 128) * scale
+    pl.semaphore_wait(barrier, len(near))
+    copies_x = [
+        send(
+            sent_x.at[pl.ds(peer[1] * 4, 4)],
+            got_x.at[mode],
+            x_send.at[d],
+            x_recv.at[d],
+            peer,
+        )
+        for d, peer in enumerate(x_peers)
+    ]
+    relay(1)
+    got_x[mode] = sent_x[pl.ds(mode * 4, 4)]
+
     def phase(order, shape):
         return order * (2 * iota(shape, 1) + 1)
 
@@ -357,6 +367,10 @@
     )
     weight = jnp.sum(weight, axis=0, keepdims=True) * (2.0 / NLAT / 16.0)
 
+    for p in range(2):
+        for table, flipped in ((cos_high, flip_high), (cos_low, flip_low)):
+            for block in range(0, PAIRS, 128):
+                flipped[p, :, block : block + 128] = table[p, block : block + 128, :].T
     receive(copies_x)
     even_rows = (iota((32, 1), 0) & 4) == 0
     field_rows = iota((32, 1), 0) & 3
@@ -390,7 +404,7 @@
     )
     product = product * weight
     folded = swap(product) + sign * product
-    orders = parities(*[dot3(folded, cos_high[p], cos_low[p], True) for p in range(2)])
+    orders = parities(*[dot3(folded, flip_high[p], flip_low[p]) for p in range(2)])
 
     def contract(p):
         first = dot3(orders[:, :half], exp_high[p, :half, :half], exp_low[p, :half, :half], True)
@@ -406,48 +420,80 @@
         for d, peer in enumerate(x_peers + core_peers)
     ]
     got_n[mine] = sent_n[mode]
+    relayed(1)
+    relay(2)
+
+    loads[1].wait()
+    to_tiles(permute_lanes(previous_raw[...].reshape(48, 256), part), wide)
+    push = 4.0 * SHELLS_DEV * SHELLS_DEV
+    forcing[pl.ds(core * SHELLS_DEV, SHELLS_DEV)] = (
+        2.0 * tri_x[...] - (0.5 * push) * wide[...]
+    ).reshape(SHELLS_DEV, 8, 128)
+    copy_u = send(
+        forcing.at[pl.ds(core * SHELLS_DEV, SHELLS_DEV)],
+        forcing.at[pl.ds(core * SHELLS_DEV, SHELLS_DEV)],
+        u_send.at[0],
+        u_recv.at[0],
+        core_peers[0],
+    )
 
     loads[4].wait()
     kappa = jnp.full(TILE, 1.0, F32)
     for f in range(FIELDS):
         kappa = jnp.where(field == f, kappa_ref[f], kappa)
-    spread = kappa * (16.0 * SHELLS_DEV * SHELLS_DEV)
-    damping = kappa * (degree * (degree + 1.0)) * (1.0 / 256.0)
+    alpha = 1.0 / (kappa * (16.0 * SHELLS_DEV * SHELLS_DEV))
+    steep = 16.0 * (degree * (degree + 1.0))
+    one = jnp.ones(TILE, F32)
+    for block in range(SHELLS // 256):
+        rho = (iota((256, 128), 0) + block * 256).astype(F32) + (SHELLS + 0.5)
+        shell_q[block * 256 : (block + 1) * 256, :] = 1.0 / (rho * rho)
+
+    def beta(shell):
+        return alpha + steep * shell_q[pl.ds(shell, 1), :]
+
     first_shell = (row // 2) * CHIP
+    grow, change = one, one
+    back, back_change = one, one
     for s in range(CHIP):
-        number = jnp.full(TILE, (first_shell + s).astype(F32), F32)
-        inverse = 1.0 / (0.5 + (number + 0.5) / (2.0 * SHELLS))
-        slope = spread * (inverse * (1.0 / (2.0 * SHELLS)))
-        radial[0, s] = (1.0 + 2.0 * spread) + damping * inverse * inverse
-        radial[1, s] = spread - slope
-        radial[2, s] = spread + slope
-    cp, cq = jnp.zeros(TILE, F32), jnp.zeros(TILE, F32)
+        green[1, s] = grow
+        change = beta(first_shell + s) * grow + change
+        grow = grow + change
+        t = CHIP - 1 - s
+        green[0, t] = back
+        back_change = beta(first_shell + t) * back + back_change
+        back = back + back_change
+    inverse = 1.0 / grow
     for s in range(CHIP):
-        t = CHIP - 1 - s
-        ip = 1.0 / (radial[0, s] - radial[1, s] * cp)
-        cp = radial[2, s] * ip
-        radial[3, s], radial[4, s] = cp, ip
-        iq = 1.0 / (radial[0, t] - radial[2, t] * cq)
-        cq = radial[1, t] * iq
-        radial[5, t], radial[6, t] = cq, iq
-    low_run = up_run = head_run = tail_run = jnp.ones(TILE, F32)
-    for s in range(CHIP):
-        t = CHIP - 1 - s
-        iq, ip = radial[6, s], radial[4, t]
-        green[0, s] = iq * head_run
-        head_run = head_run * (radial[2, s] * iq)
-        low_run = low_run * radial[5, s]
-        green[2, s] = low_run
-        green[1, t] = ip * tail_run
-        tail_run = tail_run * (radial[1, t] * ip)
-        up_run = up_run * radial[3, t]
-        green[3, t] = up_run
-    port_z[z, 0], port_z[z, 1] = green[2, 0], green[3, 0]
-    port_z[z, 2], port_z[z, 3] = green[2, CHIP - 1], green[3, CHIP - 1]
-    copies_pz = [
-        send(port_z.at[z], port_z.at[z], pz_send.at[d], pz_recv.at[d], peer)
-        for d, peer in enumerate(z_peers)
-    ]
+        green[0, s] = green[0, s] * inverse
+        green[1, s] = green[1, s] * inverse
+
+    def line_ports(line):
+        starts = [line * 256 + k * CHIP for k in range(8)]
+        carry = []
+        for start in starts:
+            change = beta(start) + one
+            carry += [one + change, change, one, one]
+
+        def step(s, carry):
+            after = []
+            for k, start in enumerate(starts):
+                grow, change, inner, inner_change = carry[4 * k : 4 * k + 4]
+                here = beta(start + s)
+                change = here * grow + change
+                inner_change = here * inner + inner_change
+                after += [grow + change, change, inner + inner_change, inner_change]
+            return tuple(after)
+
+        carry = lax.fori_loop(1, CHIP, step, tuple(carry))
+        ports = []
+        for k in range(8):
+            grow, change, inner, _ = carry[4 * k : 4 * k + 4]
+            tau = 1.0 / grow
+            ports.append((inner * tau, tau, tau, (grow - change) * tau))
+        return ports
+
+    parts_z = level_parts(line_ports(y), z)
+    port_y[y, 0], port_y[y, 1], port_y[y, 2] = parts_z[4][0], parts_z[4][1], parts_z[4][3]
 
     loads[2].wait()
     loads[3].wait()
@@ -459,13 +505,21 @@
         jnp.concatenate([parted[k * 8 : k * 8 + 4, :128], parted[k * 8 : k * 8 + 4, 128:]], axis=0)
         for k in range(2)
     ]
+    bottom, top = bottom * (SHELLS - 0.5), top * (2 * SHELLS + 0.5)
+
+    relayed(2)
+    copies_py = [
+        send(port_y.at[y], port_y.at[y], py_send.at[d], py_recv.at[d], peer)
+        for d, peer in enumerate(y_peers)
+    ]
 
     receive([copy_u])
     receive(copies_n)
     factor = (1.5 * push) * scale
     sums = [[None] * 4, [None] * 4]
     for s in range(CHIP):
-        value = forcing[s] + factor * got_n[s // 4, s % 4]
+        rho = (first_shell + s).astype(F32) + (SHELLS + 0.5)
+        value = (alpha * rho) * (forcing[s] + factor * got_n[s // 4, s % 4])
         solved[s] = value
         for k in range(2):
             term = green[k, s] * value
@@ -478,24 +532,16 @@
         for d, peer in enumerate(z_peers)
     ]
 
-    receive(copies_pz)
-    parts_z = level_parts([tuple(port_z[k, m] for m in range(4)) for k in range(8)], z)
-    for m in range(4):
-        port_y[y, m] = parts_z[4][m]
-    copies_py = [
-        send(port_y.at[y], port_y.at[y], py_send.at[d], py_recv.at[d], peer)
-        for d, peer in enumerate(y_peers)
-    ]
-
     run = jnp.zeros(TILE, F32)
     for s in range(CHIP):
-        ip = radial[4, s]
-        run = solved[s] * ip + (radial[1, s] * ip) * run
-        solved[s] = run
+        run = run + (green[1, s] * grow) * solved[s]
+        partial[s] = green[0, s] * run
     run = jnp.zeros(TILE, F32)
     for s in reversed(range(CHIP)):
-        run = solved[s] + radial[3, s] * run
-        solved[s] = run
+        solved_here = solved[s]
+        solved[s] = partial[s] + green[1, s] * run
+        run = run + (green[0, s] * grow) * solved_here
+
     for q in range(4):
         wide[q * 32 : (q + 1) * 32, :] = (got_n[core * 4 + q] * scale).reshape(32, 128)
     nonlinear_ref[...] = permute_lanes(from_tiles(wide), unite).reshape(FIELDS, SHELLS_DEV, 256)
@@ -510,12 +556,16 @@
         for d, peer in enumerate(y_peers)
     ]
 
+    own_shells = pl.ds(core * SHELLS_DEV, SHELLS_DEV)
+    number = (row * SHELLS_DEV + iota((SHELLS_DEV, 8, 128), 0)).astype(F32) + (SHELLS + 0.5)
+    over = 1.0 / number
+    rest = solved[own_shells] * over - tri_x[...].reshape(SHELLS_DEV, 8, 128)
+    from_low, from_up = green[0, own_shells] * over, green[1, own_shells] * over
+
     receive(copies_py)
-    parts_y = level_parts([tuple(port_y[k, m] for m in range(4)) for k in range(8)], y)
-    own_shells = pl.ds(core * SHELLS_DEV, SHELLS_DEV)
-    rest = solved[own_shells] - tri_x[...].reshape(SHELLS_DEV, 8, 128)
-    from_low, from_up = green[2, own_shells], green[3, own_shells]
-
+    parts_y = level_parts(
+        [(port_y[k, 0], port_y[k, 1], port_y[k, 1], port_y[k, 2]) for k in range(8)], y
+    )
     receive(copies_cy)
     _, _, lower_y, upper_y = level_constants(
         parts_y, [(const_y[k, 0], const_y[k, 1]) for k in range(8)], y
@@ -527,7 +577,7 @@
     wide[...] = (rest + from_low * chip_low + from_up * chip_up).reshape(128, 128)
     new_ref[...] = permute_lanes(from_tiles(wide), unite).reshape(FIELDS, SHELLS_DEV, 256)
 
-    for copy in copies_x + copies_n + [copy_u] + copies_pz + copies_py + copies_cz + copies_cy:
+    for copy in copies_x + copies_n + [copy_u] + copies_py + copies_cz + copies_cy:
         copy.wait_send()
 
 
@@ -566,15 +616,18 @@
         vmem((2, 56, HALF), F32),
         vmem((2, PAIRS, HALF), BF16),
         vmem((2, PAIRS, HALF), BF16),
+        vmem((2, HALF, PAIRS), BF16),
+        vmem((2, HALF, PAIRS), BF16),
         vmem((4, 4, 8, 128), F32),
         vmem((8, 4, 8, 128), F32),
-        vmem((7, CHIP, 8, 128), F32),
-        vmem((4, CHIP, 8, 128), F32),
+        vmem((SHELLS, 128), F32),
         vmem((CHIP, 8, 128), F32),
-        vmem((8, 4, 8, 128), F32),
-        vmem((8, 4, 8, 128), F32),
+        vmem((2, CHIP, 8, 128), F32),
+        vmem((CHIP, 8, 128), F32),
+        vmem((8, 3, 8, 128), F32),
         vmem((8, 2, 8, 128), F32),
         vmem((8, 2, 8, 128), F32),
+        pltpu.SemaphoreType.REGULAR((2, 2, 2)),
         dma((5,)),
         dma((3,)),
         dma((3,)),
@@ -582,7 +635,7 @@
         dma((7,)),
         dma((1,)),
         dma((1,)),
-    ] + [dma((7,))] * 8
+    ] + [dma((7,))] * 6
     held = pltpu.VMEM(state.shape, F32)
     operands = [
         pltpu.with_memory_space_constraint(operand, pltpu.HBM)

time: 35.7 us -> 34.6 us (0.969)
  Pallas kernels: 34.8 us -> 33.8 us
    pallas_call x1, Pallas kernels: 34.2 us -> 33.2 us  [local(): pl.pallas_call(kernel, out_shape=(held, held), in_specs=[anywhere] * 5, o...]
where the time goes in v2:
time: 34.6 us; the launch traced here: 34.4 us
  Pallas kernels  33.8 us (98%)
  between operations  0.64 us (2%)
    pallas_call x1, Pallas kernels, local(): pl.pallas_call(kernel, out_shape=(held, held), in_specs=[anywhere] * 5, o...  33.2 us

profile of v2, /device:TPU:1, one launch (start us, length us, event | category | flops | bytes accessed | tf_op | source)
XLA Modules:
  0.0 34.4 jit_solution(10149743031258218572)
XLA Ops:
  0.6 33.2 %shard_map.68 = (f32[3,16,256]{2,1,0:T(8,128)S(1)}, f32[3,16,256]{2,1,0:T(8,128)S(1)}) custom-call(f32[3,16,256]{2,1,0:T(8,128)} %state_hbm.1, f32[3,16,256]{2,1,0:T(8,128)} %previous_hbm.1, f32[3,2,256]{2,1,0:T(2,128)} %bitcast.2, f32[3,2,256]{2,1,0:T(2,128)} %bitcast.3, f32[3]{0:T(128)} %kappa_hbm.1), custom_call_target="tpu_custom_call" | custom-call | tf_op jit(solution)/shard_map/pallas_call | solution.py:650
  33.8 0.7 %shard_map.69 = (f32[3,16,256]{2,1,0:T(8,128)}, f32[3,16,256]{2,1,0:T(8,128)}) custom-call(f32[3,16,256]{2,1,0:T(8,128)S(1)} %get-tuple-element.4.new_ref, f32[3,16,256]{2,1,0:T(8,128)S(1)} %get-tuple-element.5.nonlinear_ref), custom_call_target="tpu_custom_call" | custom-call | tf_op jit(solution)/shard_map/pallas_call | solution.py:660

commit v3 on v2

--- a/solution.py
+++ b/solution.py
@@ -169,10 +169,13 @@
     angle_sin,
     cos_high,
     cos_low,
+    leg_high,
+    leg_low,
     flip_high,
     flip_low,
     sent_n,
     got_n,
+    spread_n,
     shell_q,
     partial,
     green,
@@ -283,6 +286,38 @@
             axis=0,
         )
 
+    def phase(order, shape):
+        return order * (2 * iota(shape, 1) + 1)
+
+    wide_shape = (8, HALF)
+    for p, groups in ((0, 7), (1, 4)):
+        for group in range(groups):
+            turns = phase(32 * (group * 8 + iota(wide_shape, 0)) + p, wide_shape)
+            angle_cos[p, group * 8 : group * 8 + 8, :] = 2.0 * cosine(turns)
+            angle_sin[p, group * 8 : group * 8 + 8, :] = 2.0 * cosine(turns - NLAT)
+    tri_x[...] = jnp.zeros_like(tri_x)
+    spread_n[...] = jnp.zeros_like(spread_n)
+    wide[...] = jnp.zeros_like(wide)
+    loads[0].wait()
+    to_tiles(permute_lanes(state_raw[...].reshape(48, 256), part), tri_x)
+    wide[...] = (tri_x[...].reshape(SHELLS_DEV, 8, 128) * scale).reshape(128, 128)
+    for k in range(4):
+        for f in range(FIELDS):
+            sent_x[k, f] = wide[pl.ds(k * 32 + f, 8, stride=4), :]
+    pl.semaphore_wait(barrier, len(near))
+    copies_x = [
+        send(
+            sent_x.at[peer[1]],
+            got_x.at[mode],
+            x_send.at[d],
+            x_recv.at[d],
+            peer,
+        )
+        for d, peer in enumerate(x_peers)
+    ]
+    relay(1)
+    got_x[mode] = sent_x[mode]
+
     toeplitz = central_ratio(512 + iota((8, 640), 0) - iota((8, 640), 1))
     hankel = [central_ratio(iota((8, 1024), 0) + iota((8, 1024), 1) + p) for p in range(2)]
     for step in range(16):
@@ -305,34 +340,6 @@
                 exp_high[here] = high
                 exp_low[here] = low
 
-    tri_x[...] = jnp.zeros_like(tri_x)
-    wide[...] = jnp.zeros_like(wide)
-    loads[0].wait()
-    to_tiles(permute_lanes(state_raw[...].reshape(48, 256), part), tri_x)
-    sent_x[...] = tri_x[...].reshape(SHELLS_DEV, 8, 128) * scale
-    pl.semaphore_wait(barrier, len(near))
-    copies_x = [
-        send(
-            sent_x.at[pl.ds(peer[1] * 4, 4)],
-            got_x.at[mode],
-            x_send.at[d],
-            x_recv.at[d],
-            peer,
-        )
-        for d, peer in enumerate(x_peers)
-    ]
-    relay(1)
-    got_x[mode] = sent_x[pl.ds(mode * 4, 4)]
-
-    def phase(order, shape):
-        return order * (2 * iota(shape, 1) + 1)
-
-    wide_shape = (8, HALF)
-    for p, groups in ((0, 7), (1, 4)):
-        for group in range(groups):
-            turns = phase(32 * (group * 8 + iota(wide_shape, 0)) + p, wide_shape)
-            angle_cos[p, group * 8 : group * 8 + 8, :] = 2.0 * cosine(turns)
-            angle_sin[p, group * 8 : group * 8 + 8, :] = 2.0 * cosine(turns - NLAT)
     base_shape = (16, HALF)
     turns = phase(2 * iota(base_shape, 0), base_shape)
     base_cos, base_sin = cosine(turns), cosine(turns - NLAT)
@@ -368,52 +375,46 @@
     weight = jnp.sum(weight, axis=0, keepdims=True) * (2.0 / NLAT / 16.0)
 
     for p in range(2):
-        for table, flipped in ((cos_high, flip_high), (cos_low, flip_low)):
-            for block in range(0, PAIRS, 128):
-                flipped[p, :, block : block + 128] = table[p, block : block + 128, :].T
+        for first in (0, 256):
+            rows, depth = slice(first, first + 256), first + 256
+            top, rest = exp_high[p, rows, :depth], exp_low[p, rows, :depth]
+            both = dot(jnp.concatenate([top, rest], axis=0), cos_high[p, :depth, :])
+            values = both[:256] + both[256:] + dot(top, cos_low[p, :depth, :])
+            for part_of, table, flipped in zip(
+                split2(values), (leg_high, leg_low), (flip_high, flip_low)
+            ):
+                table[p, rows, :] = part_of
+                flipped[p, :, rows] = part_of.T
+
     receive(copies_x)
-    even_rows = (iota((32, 1), 0) & 4) == 0
-    field_rows = iota((32, 1), 0) & 3
+    even_rows = (iota((32, 1), 0) & 1) == 0
     sign = jnp.where(even_rows, 1.0, -1.0)
 
     def parities(left, right):
         return jnp.where(even_rows, left, right)
 
     def swap(values):
-        return pltpu.roll(values.reshape(4, 8, values.shape[1]), 4, 1).reshape(values.shape)
-
-    def rolled(values, shift):
-        return pltpu.roll(values.reshape(4, 8, values.shape[1]), shift, 1).reshape(values.shape)
-
-    spectrum = jnp.concatenate([got_x[k].reshape(32, 128) for k in range(4)], axis=1)
-    half = PAIRS // 2
-
-    def expand(p):
-        first = dot3(spectrum, exp_high[p, :, :half], exp_low[p, :, :half])
-        second = dot3(spectrum[:, half:], exp_high[p, half:, half:], exp_low[p, half:, half:])
-        return jnp.concatenate([first, second], axis=1)
-
-    orders = parities(expand(0), expand(1))
-    sides = parities(*[dot3(orders, cos_high[p], cos_low[p]) for p in range(2)])
+        rows = values.shape[0]
+        return parities(pltpu.roll(values, rows - 1, 0), pltpu.roll(values, 1, 0))
+
+    spectrum = jnp.concatenate([jnp.concatenate([got_x[k].reshape(24, 128), jnp.zeros(TILE, F32)], axis=0)
+            for k in range(4)], axis=1)
+    sides = parities(*[dot3(spectrum, leg_high[p], leg_low[p]) for p in range(2)])
     grid = swap(sides) + sign * sides
-    after, before, twice = rolled(grid, 7), rolled(grid, 1), rolled(grid, 2)
-    product = jnp.where(
-        field_rows == 0,
-        after * after - grid * grid,
-        jnp.where(field_rows == 1, before * grid, jnp.where(field_rows == 2, -(twice * grid), 0.0)),
-    )
-    product = product * weight
+    velocity, magnetic, thermal = [grid[f * 8 : f * 8 + 8] * weight for f in range(FIELDS)]
+    product = jnp.concatenate(
+        [
+            grid[8:16] * magnetic - grid[:8] * velocity,
+            grid[:8] * magnetic,
+            -(grid[:8] * thermal),
+            jnp.zeros_like(thermal),
+        ],
+        axis=0,
+    )
     folded = swap(product) + sign * product
-    orders = parities(*[dot3(folded, flip_high[p], flip_low[p]) for p in range(2)])
-
-    def contract(p):
-        first = dot3(orders[:, :half], exp_high[p, :half, :half], exp_low[p, :half, :half], True)
-        second = dot3(orders, exp_high[p, half:, :], exp_low[p, half:, :], True)
-        return jnp.concatenate([first, second], axis=1)
-
-    terms = parities(contract(0), contract(1))
+    terms = parities(*[dot3(folded, flip_high[p], flip_low[p]) for p in range(2)])
     for k in range(4):
-        sent_n[k] = terms[:, k * 128 : (k + 1) * 128].reshape(4, 8, 128)
+        sent_n[k] = terms[:24, k * 128 : (k + 1) * 128].reshape(FIELDS, 8, 128)
     mine = core * 4 + mode
     copies_n = [
         send(sent_n.at[peer[1]], got_n.at[mine], n_send.at[d], n_recv.at[d], peer)
@@ -515,11 +516,14 @@
 
     receive([copy_u])
     receive(copies_n)
+    for q in range(8):
+        for f in range(FIELDS):
+            spread_n[pl.ds(q * 32 + f, 8, stride=4), :] = got_n[q, f]
     factor = (1.5 * push) * scale
     sums = [[None] * 4, [None] * 4]
     for s in range(CHIP):
         rho = (first_shell + s).astype(F32) + (SHELLS + 0.5)
-        value = (alpha * rho) * (forcing[s] + factor * got_n[s // 4, s % 4])
+        value = (alpha * rho) * (forcing[s] + factor * spread_n[s * 8 : s * 8 + 8, :])
         solved[s] = value
         for k in range(2):
             term = green[k, s] * value
@@ -542,8 +546,9 @@
         solved[s] = partial[s] + green[1, s] * run
         run = run + (green[0, s] * grow) * solved_here
 
-    for q in range(4):
-        wide[q * 32 : (q + 1) * 32, :] = (got_n[core * 4 + q] * scale).reshape(32, 128)
+    wide[...] = (
+        spread_n[pl.ds(core * 128, 128), :].reshape(SHELLS_DEV, 8, 128) * scale
+    ).reshape(128, 128)
     nonlinear_ref[...] = permute_lanes(from_tiles(wide), unite).reshape(FIELDS, SHELLS_DEV, 256)
 
     receive(copies_cz)
@@ -605,8 +610,8 @@
         vmem((16, 256), F32),
         vmem((128, 128), F32),
         vmem((128, 128), F32),
-        vmem((16, 8, 128), F32),
-        vmem((4, 4, 8, 128), F32),
+        vmem((4, FIELDS, 8, 128), F32),
+        vmem((4, FIELDS, 8, 128), F32),
         vmem((CHIP, 8, 128), F32),
         vmem((4, 128, 128), F32),
         vmem((2, 7, 128, 128), F32),
@@ -616,10 +621,13 @@
         vmem((2, 56, HALF), F32),
         vmem((2, PAIRS, HALF), BF16),
         vmem((2, PAIRS, HALF), BF16),
+        vmem((2, PAIRS, HALF), BF16),
+        vmem((2, PAIRS, HALF), BF16),
         vmem((2, HALF, PAIRS), BF16),
         vmem((2, HALF, PAIRS), BF16),
-        vmem((4, 4, 8, 128), F32),
-        vmem((8, 4, 8, 128), F32),
+        vmem((4, FIELDS, 8, 128), F32),
+        vmem((8, FIELDS, 8, 128), F32),
+        vmem((CHIP * 8, 128), F32),
         vmem((SHELLS, 128), F32),
         vmem((CHIP, 8, 128), F32),
         vmem((2, CHIP, 8, 128), F32),

time: 34.6 us -> 34 us (0.983)
  Pallas kernels: 33.8 us -> 33.2 us
    pallas_call x1, Pallas kernels: 33.2 us -> 32.6 us  [local(): pl.pallas_call(kernel, out_shape=(held, held), in_specs=[anywhere] * 5, o...]
where the time goes in v3:
time: 34 us; the launch traced here: 33.9 us
  Pallas kernels  33.2 us (98%)
  between operations  0.64 us (2%)
    pallas_call x1, Pallas kernels, local(): pl.pallas_call(kernel, out_shape=(held, held), in_specs=[anywhere] * 5, o...  32.6 us

profile of v3, /device:TPU:1, one launch (start us, length us, event | category | flops | bytes accessed | tf_op | source)
XLA Modules:
  0.0 33.9 jit_solution(4176208302045362023)
XLA Ops:
  0.6 32.6 %shard_map.68 = (f32[3,16,256]{2,1,0:T(8,128)S(1)}, f32[3,16,256]{2,1,0:T(8,128)S(1)}) custom-call(f32[3,16,256]{2,1,0:T(8,128)} %state_hbm.1, f32[3,16,256]{2,1,0:T(8,128)} %previous_hbm.1, f32[3,2,256]{2,1,0:T(2,128)} %bitcast.2, f32[3,2,256]{2,1,0:T(2,128)} %bitcast.3, f32[3]{0:T(128)} %kappa_hbm.1), custom_call_target="tpu_custom_call" | custom-call | tf_op jit(solution)/shard_map/pallas_call | solution.py:658
  33.2 0.7 %shard_map.69 = (f32[3,16,256]{2,1,0:T(8,128)}, f32[3,16,256]{2,1,0:T(8,128)}) custom-call(f32[3,16,256]{2,1,0:T(8,128)S(1)} %get-tuple-element.4.new_ref, f32[3,16,256]{2,1,0:T(8,128)S(1)} %get-tuple-element.5.nonlinear_ref), custom_call_target="tpu_custom_call" | custom-call | tf_op jit(solution)/shard_map/pallas_call | solution.py:668

commit v4 on v3

--- a/solution.py
+++ b/solution.py
@@ -343,36 +343,28 @@
     base_shape = (16, HALF)
     turns = phase(2 * iota(base_shape, 0), base_shape)
     base_cos, base_sin = cosine(turns), cosine(turns - NLAT)
-    base_row = iota((16, 128), 0)
-
-    def series_term(q):
-        order = (16 * q + base_row).astype(F32)
-        term = -1.0 / (4.0 * order * order - 1.0)
-        term = jnp.where(order > HALF, 0.0, term)
-        return jnp.concatenate([term] * (HALF // 128), axis=1)
-
-    def table_rows(p, q):
-        return (
-            angle_cos[p, pl.ds(q, 1), :] * base_cos - angle_sin[p, pl.ds(q, 1), :] * base_sin
-        )
-
-    def fill(q, weight):
+    def fill(q, unused):
         for p in range(2):
-            values = table_rows(p, q)
+            row_cos, row_sin = angle_cos[p, pl.ds(q, 1), :], angle_sin[p, pl.ds(q, 1), :]
+            values = row_cos * base_cos - row_sin * base_sin
             if p == 0:
                 values = jnp.where((iota(base_shape, 0) + 16 * q) == 0, 1.0, values)
-                weight = weight + series_term(q) * values
             high, low = split2(values)
             where = pl.ds(pl.multiple_of(q * 16, 16), 16)
             cos_high[p, where, :] = high
             cos_low[p, where, :] = low
-        return weight
-
-    weight = lax.fori_loop(0, 32, fill, jnp.zeros(base_shape, F32))
-    weight = lax.fori_loop(
-        32, 49, lambda q, weight: weight + series_term(q) * table_rows(0, q), weight
-    )
-    weight = jnp.sum(weight, axis=0, keepdims=True) * (2.0 / NLAT / 16.0)
+        return unused
+
+    lax.fori_loop(0, 32, fill, 0)
+    order = (iota((16, 56), 0) + 16 * iota((16, 56), 1)).astype(F32)
+    series = jnp.where(order > HALF, 0.0, -1.0 / (4.0 * order * order - 1.0))
+    series = jnp.where(order == 0.0, 0.5, series)
+    over_cos, over_sin = [
+        jnp.dot(series, rows[0], precision=lax.Precision.HIGHEST, preferred_element_type=F32)
+        for rows in (angle_cos, angle_sin)
+    ]
+    weight = jnp.sum(over_cos * base_cos - over_sin * base_sin, axis=0, keepdims=True)
+    weight = weight * (2.0 / NLAT / 16.0)
 
     for p in range(2):
         for first in (0, 256):

time: 34 us -> 33.5 us (0.985)
  Pallas kernels: 33.2 us -> 32.7 us
    pallas_call x1, Pallas kernels: 32.6 us -> 32.1 us  [local(): pl.pallas_call(kernel, out_shape=(held, held), in_specs=[anywhere] * 5, o...]
where the time goes in v4:
time: 33.5 us; the launch traced here: 33.4 us
  Pallas kernels  32.7 us (98%)
  between operations  0.64 us (2%)
    pallas_call x1, Pallas kernels, local(): pl.pallas_call(kernel, out_shape=(held, held), in_specs=[anywhere] * 5, o...  32.1 us

profile of v4, /device:TPU:1, one launch (start us, length us, event | category | flops | bytes accessed | tf_op | source)
XLA Modules:
  0.0 33.4 jit_solution(1691779022013289271)
XLA Ops:
  0.6 32.1 %shard_map.68 = (f32[3,16,256]{2,1,0:T(8,128)S(1)}, f32[3,16,256]{2,1,0:T(8,128)S(1)}) custom-call(f32[3,16,256]{2,1,0:T(8,128)} %state_hbm.1, f32[3,16,256]{2,1,0:T(8,128)} %previous_hbm.1, f32[3,2,256]{2,1,0:T(2,128)} %bitcast.2, f32[3,2,256]{2,1,0:T(2,128)} %bitcast.3, f32[3]{0:T(128)} %kappa_hbm.1), custom_call_target="tpu_custom_call" | custom-call | tf_op jit(solution)/shard_map/pallas_call | solution.py:650
  32.7 0.7 %shard_map.69 = (f32[3,16,256]{2,1,0:T(8,128)}, f32[3,16,256]{2,1,0:T(8,128)}) custom-call(f32[3,16,256]{2,1,0:T(8,128)S(1)} %get-tuple-element.4.new_ref, f32[3,16,256]{2,1,0:T(8,128)S(1)} %get-tuple-element.5.nonlinear_ref), custom_call_target="tpu_custom_call" | custom-call | tf_op jit(solution)/shard_map/pallas_call | solution.py:660

commit v5 on v4

--- a/solution.py
+++ b/solution.py
@@ -202,8 +202,8 @@
     y, z, core = row // 16, lax.rem(row // 2, 8), lax.rem(row, 2)
     other = row + 1 - 2 * core
     turn = [lax.rem(mode + d, 4) for d in range(4)]
-    x_peers = [(row, turn[d]) for d in range(1, 4)]
-    core_peers = [(other, turn[d]) for d in range(4)]
+    x_peers = [(row, turn[d]) for d in (2, 1, 3)]
+    core_peers = [(other, turn[d]) for d in (2, 1, 3, 0)]
 
     loads = [
         pltpu.make_async_copy(state_hbm, state_raw, load_sem.at[0]),
@@ -295,6 +295,17 @@
             turns = phase(32 * (group * 8 + iota(wide_shape, 0)) + p, wide_shape)
             angle_cos[p, group * 8 : group * 8 + 8, :] = 2.0 * cosine(turns)
             angle_sin[p, group * 8 : group * 8 + 8, :] = 2.0 * cosine(turns - NLAT)
+    toeplitz = central_ratio(512 + iota((8, 640), 0) - iota((8, 640), 1))
+    hankel = [central_ratio(iota((8, 1024), 0) + iota((8, 1024), 1) + p) for p in range(2)]
+    for step in range(16):
+        rows = slice(step * 8, step * 8 + 8)
+        moved = toeplitz if step == 0 else pltpu.roll(toeplitz, step * 8, 1)
+        for b in range(4):
+            ports_t[b, rows, :] = moved[:, (4 - b) * 128 : (5 - b) * 128]
+        for p in range(2):
+            moved = hankel[p] if step == 0 else pltpu.roll(hankel[p], 1024 - step * 8, 1)
+            for b in range(7):
+                ports_h[p, b, rows, :] = moved[:, b * 128 : (b + 1) * 128]
     tri_x[...] = jnp.zeros_like(tri_x)
     spread_n[...] = jnp.zeros_like(spread_n)
     wide[...] = jnp.zeros_like(wide)
@@ -318,17 +329,6 @@
     relay(1)
     got_x[mode] = sent_x[mode]
 
-    toeplitz = central_ratio(512 + iota((8, 640), 0) - iota((8, 640), 1))
-    hankel = [central_ratio(iota((8, 1024), 0) + iota((8, 1024), 1) + p) for p in range(2)]
-    for step in range(16):
-        rows = slice(step * 8, step * 8 + 8)
-        moved = toeplitz if step == 0 else pltpu.roll(toeplitz, step * 8, 1)
-        for b in range(4):
-            ports_t[b, rows, :] = moved[:, (4 - b) * 128 : (5 - b) * 128]
-        for p in range(2):
-            moved = hankel[p] if step == 0 else pltpu.roll(hankel[p], 1024 - step * 8, 1)
-            for b in range(7):
-                ports_h[p, b, rows, :] = moved[:, b * 128 : (b + 1) * 128]
     for p in range(2):
         for a in range(4):
             for b in range(4):
@@ -410,7 +410,7 @@
     mine = core * 4 + mode
     copies_n = [
         send(sent_n.at[peer[1]], got_n.at[mine], n_send.at[d], n_recv.at[d], peer)
-        for d, peer in enumerate(x_peers + core_peers)
+        for d, peer in enumerate(x_peers[:1] + core_peers[:1] + x_peers[1:] + core_peers[1:])
     ]
     got_n[mine] = sent_n[mode]
     relayed(1)
@@ -427,7 +427,7 @@
         forcing.at[pl.ds(core * SHELLS_DEV, SHELLS_DEV)],
         u_send.at[0],
         u_recv.at[0],
-        core_peers[0],
+        core_peers[3],
     )
 
     loads[4].wait()
@@ -556,8 +556,14 @@
     own_shells = pl.ds(core * SHELLS_DEV, SHELLS_DEV)
     number = (row * SHELLS_DEV + iota((SHELLS_DEV, 8, 128), 0)).astype(F32) + (SHELLS + 0.5)
     over = 1.0 / number
-    rest = solved[own_shells] * over - tri_x[...].reshape(SHELLS_DEV, 8, 128)
-    from_low, from_up = green[0, own_shells] * over, green[1, own_shells] * over
+    ordered = []
+    for values in (
+        solved[own_shells] * over - tri_x[...].reshape(SHELLS_DEV, 8, 128),
+        green[0, own_shells] * over,
+        green[1, own_shells] * over,
+    ):
+        wide[...] = values.reshape(128, 128)
+        ordered.append(permute_lanes(from_tiles(wide), unite))
 
     receive(copies_py)
     parts_y = level_parts(
@@ -571,8 +577,18 @@
     line_up = parts_y[3][0] * bottom + parts_y[3][1] * top + upper_y
     chip_low = parts_z[2][0] * line_low + parts_z[2][1] * line_up + lower_z
     chip_up = parts_z[3][0] * line_low + parts_z[3][1] * line_up + upper_z
-    wide[...] = (rest + from_low * chip_low + from_up * chip_up).reshape(128, 128)
-    new_ref[...] = permute_lanes(from_tiles(wide), unite).reshape(FIELDS, SHELLS_DEV, 256)
+    edges = [
+        jnp.concatenate([tile[:4], tile[4:]], axis=1)
+        for tile in (chip_low, chip_up, jnp.zeros(TILE, F32), jnp.zeros(TILE, F32))
+    ]
+    edges = permute_lanes(jnp.concatenate(edges, axis=0), unite)
+    for f in range(FIELDS):
+        rows = slice(f * SHELLS_DEV, (f + 1) * SHELLS_DEV)
+        new_ref[f] = (
+            ordered[0][rows]
+            + ordered[1][rows] * edges[f : f + 1]
+            + ordered[2][rows] * edges[4 + f : 5 + f]
+        )
 
     for copy in copies_x + copies_n + [copy_u] + copies_py + copies_cz + copies_cy:
         copy.wait_send()

time: 33.5 us -> 33.1 us (0.988)
  Pallas kernels: 32.7 us -> 32.3 us
    pallas_call x1, Pallas kernels: 32.1 us -> 31.7 us  [local(): pl.pallas_call(kernel, out_shape=(held, held), in_specs=[anywhere] * 5, o...]
where the time goes in v5:
time: 33.1 us; the launch traced here: 32.9 us
  Pallas kernels  32.3 us (98%)
  between operations  0.64 us (2%)
    pallas_call x1, Pallas kernels, local(): pl.pallas_call(kernel, out_shape=(held, held), in_specs=[anywhere] * 5, o...  31.7 us

profile of v5, /device:TPU:1, one launch (start us, length us, event | category | flops | bytes accessed | tf_op | source)
XLA Modules:
  0.0 32.9 jit_solution(15915531851093021432)
XLA Ops:
  0.6 31.7 %shard_map.68 = (f32[3,16,256]{2,1,0:T(8,128)S(1)}, f32[3,16,256]{2,1,0:T(8,128)S(1)}) custom-call(f32[3,16,256]{2,1,0:T(8,128)} %state_hbm.1, f32[3,16,256]{2,1,0:T(8,128)} %previous_hbm.1, f32[3,2,256]{2,1,0:T(2,128)} %bitcast.2, f32[3,2,256]{2,1,0:T(2,128)} %bitcast.3, f32[3]{0:T(128)} %kappa_hbm.1), custom_call_target="tpu_custom_call" | custom-call | tf_op jit(solution)/shard_map/pallas_call | solution.py:666
  32.3 0.7 %shard_map.69 = (f32[3,16,256]{2,1,0:T(8,128)}, f32[3,16,256]{2,1,0:T(8,128)}) custom-call(f32[3,16,256]{2,1,0:T(8,128)S(1)} %get-tuple-element.4.new_ref, f32[3,16,256]{2,1,0:T(8,128)S(1)} %get-tuple-element.5.nonlinear_ref), custom_call_target="tpu_custom_call" | custom-call | tf_op jit(solution)/shard_map/pallas_call | solution.py:676
